TPU v7x, 32 devices: a whole 2x2x4 slice. The times are simulated.
32 devices in a mesh: groups: 2 (over y), seq: 4 (over z), mp: 2 (over x), rep: 2 (over core).
Axes of the slice: x: 2, y: 2, z: 4, core: 2. Of those that a mesh axis runs over, the one named last changes fastest.
Arguments:
- grad_hidden: bfloat16 [240, 24576], P(('groups', 'mp', 'rep'), 'seq'), parts along dimension 0, may hold values from -6 to 6
- w_up: bfloat16 [8192, 24576], P(('mp', 'rep'), 'seq'), may hold values from -0.0390625 to 0.0390625
- pool_a: bfloat16 [8, 8192, 64], P(('groups', 'seq'), ('mp', 'rep')), parts along dimension 0, may hold values from -0.75 to 0.75
- pool_b: bfloat16 [8, 64, 24576], P(('groups', 'seq')), parts along dimension 0, may hold values from -0.0390625 to 0.0390625
- seg_adapter: int32 [8, 2], P('groups'), parts along dimension 0, may hold values from 0 to 3
- adapter_slot: int32 [8], P('groups'), parts along dimension 0, may hold values from 0 to 3, each once
- seg_len: int32 [8, 2], P('groups'), parts along dimension 0, may hold values from 1 to 15, as said below
Outputs:
- input_grad: bfloat16 [240, 8192], P(('groups', 'seq'), ('mp', 'rep')), parts along dimension 0
There are 2 independent parts, one for each index of `groups`. A program takes and returns all parts, laid end to end along the dimension named above; an argument that names none is the same for every part. Nothing has to cross between parts.
Inputs may be any that keep to these rules, and one draw needn't show every extreme that they name: `adapter_slot`: pool slot of every adapter, each slot once; slot q is held by the pool shard q. `seg_len`: valid tokens stand first in their segment.
All inputs are finite; a program needn't handle non-finite values.
Results may differ from a plain program's by a relative error of at most 0.0029.
Values may be sent and summed in bfloat16 or wider, within the bound.
A program may use at most 128 MiB of HBM per device.

v0:
```python
import jax
import jax.numpy as jnp
from jax import lax
from jax.sharding import PartitionSpec as P

R = 64
TOK_DEV = 30
SEGS_BLK = 2
SEG = 15


adapter_scale_factor = 0.5


def on_device(grad_hidden, w_up, pool_a, pool_b, seg_adapter, adapter_slot, seg_len):
    pool_total = adapter_slot.shape[0]
    width_portion = pool_a.shape[1]
    matches = seg_adapter[:, :, None] == jnp.arange(pool_total, dtype=jnp.int32)[None, None, :]
    slot_ids = jnp.sum(jnp.where(matches, adapter_slot[None, None, :], 0), axis=-1)
    gathered = lax.all_gather(grad_hidden, ("mp", "rep"), axis=0, tiled=True)
    hidden_part = gathered.shape[1]
    position = jnp.arange(TOK_DEV, dtype=jnp.int32)
    within = position % SEG
    length_tok = jnp.repeat(seg_len, SEG, axis=1)
    valid = (within[None, :] < length_tok).reshape(-1)
    masked = jnp.where(valid[:, None], gathered, jnp.zeros_like(gathered))
    token_count = masked.shape[0]
    up_factor_columns = lax.all_to_all(pool_b, "seq", split_axis=2, concat_axis=0, tiled=True)
    flat_slots = slot_ids.reshape(-1)
    token_slots = jnp.repeat(flat_slots, SEG)
    all_columns = up_factor_columns.reshape(pool_total * R, hidden_part)
    every_adapter = jnp.einsum("tf,kf->tk", masked, all_columns, preferred_element_type=jnp.float32)
    every_adapter = every_adapter.reshape(token_count, pool_total, R)
    slot_match = token_slots[:, None] == jnp.arange(pool_total, dtype=jnp.int32)[None, :]
    picked = jnp.sum(jnp.where(slot_match[:, :, None], every_adapter, 0.0), axis=1)
    reduced_rank_part = adapter_scale_factor * picked
    low_mine = lax.psum_scatter(reduced_rank_part, "seq", scatter_dimension=0, tiled=True).astype(
        jnp.bfloat16
    )
    block_index = lax.axis_index("seq")
    my_slots = lax.dynamic_slice_in_dim(slot_ids, block_index, 1, 0).reshape(-1)
    empty = jnp.zeros((SEGS_BLK, width_portion, R), jnp.bfloat16)
    shard_rows = lax.all_gather(pool_a, "seq", axis=0, tiled=True)
    shard_count = shard_rows.shape[0]
    inside = (my_slots >= 0) & (my_slots < shard_count)
    taken_rows = jnp.take(shard_rows, jnp.clip(my_slots, 0, shard_count - 1), axis=0)
    a_mine = jnp.where(inside[:, None, None], taken_rows, empty)
    frozen_term = lax.psum_scatter(
        jnp.einsum("tf,df->td", masked, w_up, preferred_element_type=jnp.float32),
        "seq",
        scatter_dimension=0,
        tiled=True,
    )
    low_term = jnp.einsum(
        "jsr,jdr->jsd",
        low_mine.reshape(SEGS_BLK, SEG, R),
        a_mine,
        preferred_element_type=jnp.float32,
    )
    total = frozen_term + low_term.reshape(TOK_DEV, width_portion)
    return total.astype(jnp.bfloat16)


def solution(mesh):
    in_specs = (
        P(("groups", "mp", "rep"), "seq"),
        P(("mp", "rep"), "seq"),
        P(("groups", "seq"), ("mp", "rep"), None),
        P(("groups", "seq"), None, None),
        P("groups", None),
        P("groups"),
        P("groups", None),
    )
    out_specs = P(("groups", "seq"), ("mp", "rep"))
    return jax.shard_map(
        on_device, mesh=mesh, in_specs=in_specs, out_specs=out_specs, check_vma=False
    )
```

profile of v0, /device:TPU:0, one launch (start us, length us, event | category | flops | bytes accessed | tf_op | source)
XLA Modules:
  0.0 336.2 jit_solution(10752231478988552378)
XLA Ops:
  6.5 0.7 all-gather.6.cloned.1.call-update
  7.3 25.2 %copy.27 = bf16[1,64,24576]{1,0,2:T(2,128)(2,1)} copy(bf16[1,64,24576]{2,1,0:T(8,128)(2,1)} %param.10) | data formatting | bytes 6291456 | tf_op args[3]
  32.5 0.5 broadcast.138
  33.0 135.0 %reduce.5 = bf16[24576,64]{1,0:T(8,128)(2,1)} reduce(bf16[24576,1,64]{2,1,0:T(2,128)(2,1)} %bitcast.33, bf16[]{:T(256)} %broadcast.138), dimensions={1}, to_apply=%bitcast.27.reduce_sub_computation | reduce | bytes 6291458
  167.9 7.8 %reshape.131 = bf16[4,2,196608]{2,1,0:T(2,128)(2,1)} reshape(bf16[24576,64]{1,0:T(8,128)(2,1)} %reduce.5) | data formatting | bytes 6291456
  175.7 6.5 %all-to-all-start = ((bf16[4,2,196608]{2,1,0:T(2,128)(2,1)}), bf16[4,2,196608]{2,1,0:T(2,128)(2,1)S(1)}, u32[]{:S(2)}, u32[]{:S(2)}) async-start(bf16[4,2,196608]{2,1,0:T(2,128)(2,1)} %reshape.131), calls=%async_computation | async-start | bytes 6291456 | tf_op jit(solution)/shard_map/all_to_all | solution.py:28
  182.2 0.7 all-gather.4.cloned.1.call-update
  183.0 0.1 copy.25
  183.2 0.1 reshape.110
  183.3 0.2 select_reduce_fusion
  183.5 0.1 copy.26
  183.6 0.1 reshape.111
  183.8 0.2 clamp_reduce_fusion
  184.1 3.0 reshape.123
  187.1 14.2 %fusion.15 = f32[120,2048]{1,0:T(8,128)} fusion(bf16[2048,6144]{1,0:T(8,128)(2,1)} %param.8, bf16[120,6144]{1,0:T(8,128)(2,1)} %reshape.123, pred[120]{0:T(512)(128)(4,1)S(1)} %lt.49), kind=kOutput, calls=%fused_computation.7 | convolution fusion | flops 3020636160 | bytes 27623544 | tf_op jit(solution)/shard_map/tf,df->td/dot_general | solution.py:49
  201.3 68.4 %all-to-all-done = bf16[4,2,196608]{2,1,0:T(2,128)(2,1)S(1)} async-done(((bf16[4,2,196608]{2,1,0:T(2,128)(2,1)}), bf16[4,2,196608]{2,1,0:T(2,128)(2,1)S(1)}, u32[]{:S(2)}, u32[]{:S(2)}) %all-to-all-start) | async-done | bytes 3145760 | tf_op jit(solution)/shard_map/all_to_all | solution.py:28
  269.7 6.6 %reshape.132 = bf16[24576,1,64]{2,1,0:T(2,128)(2,1)} reshape(bf16[4,2,196608]{2,1,0:T(2,128)(2,1)S(1)} %all-to-all-done) | data formatting | bytes 6291456
  276.3 9.4 %copy.33 = bf16[1,64,24576]{1,2,0:T(8,128)(2,1)} copy(bf16[1,64,24576]{1,0,2:T(2,128)(2,1)} %bitcast.32) | data formatting | bytes 6291456
  285.7 6.8 %copy.29 = bf16[1,64,4,6144]{3,1,2,0:T(8,128)(2,1)} copy(bf16[1,64,4,6144]{1,3,2,0:T(8,128)(2,1)} %bitcast.34) | data formatting | bytes 6291456 | tf_op jit(solution)/shard_map/all_to_all | solution.py:28
  292.6 3.1 fusion.10
  295.6 0.1 copy.30
  295.7 23.4 %fusion.29 = (f32[32,64]{1,0:T(8,128)S(1)}, f32[32,2048]{1,0:T(8,128)S(1)}) fusion(f32[120,64]{1,0:T(8,128)S(1)} %copy.30, f32[120,2048]{1,0:T(8,128)S(1)} %copy-done.1), kind=kCustom, calls=%all-reduce-scatter.2 | all-reduce-scatter fusion | flops 270337 | bytes 1284608
  319.1 1.3 collective-permute-start.1
  320.4 0.6 dynamic-slice.6
  321.7 0.2 and_reduce_fusion
  321.9 1.8 gather_fusion
  323.7 2.8 collective-permute-start
  326.5 0.2 concatenate.1
  326.8 0.3 fusion.16
  327.1 1.3 collective-permute-done
  328.4 0.2 concatenate
  328.6 0.7 fusion.21
  (34 shorter events, 0.5 us)
Async XLA Ops:
  6.5 177.6 %all-gather.6.cloned.1.call-start = ((), (), s32[]{:S(2)}) async-start(), calls=%async_computation.2 | async-start | bytes 1966080 | tf_op jit(solution)/shard_map/all_gather | solution.py:20
  175.7 7.3 %copy-start.2 = (s32[4,2]{0,1:T(2,128)S(1)}, s32[4,2]{0,1:T(2,128)}, u32[]{:S(2)}) copy-start(s32[4,2]{0,1:T(2,128)} %param.13) | copy-start | bytes 100
  175.7 7.6 %copy-start.3 = (s32[4,2]{0,1:T(2,128)S(1)}, s32[4,2]{0,1:T(2,128)}, u32[]{:S(2)}) copy-start(s32[4,2]{0,1:T(2,128)} %param.11) | copy-start | bytes 100
  175.7 7.6 %copy-start.4 = (s32[4]{0:T(128)S(1)}, s32[4]{0:T(128)}, u32[]{:S(2)}) copy-start(s32[4]{0:T(128)} %param.12) | copy-start | bytes 52
  175.7 94.0 %all-to-all-start = ((bf16[4,2,196608]{2,1,0:T(2,128)(2,1)}), bf16[4,2,196608]{2,1,0:T(2,128)(2,1)S(1)}, u32[]{:S(2)}, u32[]{:S(2)}) async-start(bf16[4,2,196608]{2,1,0:T(2,128)(2,1)} %reshape.131), calls=%async_computation | async-start | bytes 6291456 | tf_op jit(solution)/shard_map/all_to_all | solution.py:28
  182.2 139.7 %all-gather.4.cloned.1.call-start = ((), (), s32[]{:S(2)}) async-start(), calls=%async_computation.1 | async-start | bytes 1310720 | tf_op jit(solution)/shard_map/all_gather | solution.py:43
  285.7 6.8 %copy-start = (bf16[120,6144]{1,0:T(8,128)(2,1)S(1)}, bf16[120,6144]{1,0:T(8,128)(2,1)}, u32[]{:S(2)}) copy-start(bf16[120,6144]{1,0:T(8,128)(2,1)} %reshape.123) | copy-start | bytes 4423684
  292.5 3.2 copy-start.1
  292.5 27.9 %copy-start.5 = (u32[32]{0:T(128)S(1)}, u32[32]{0:T(128)}, u32[]{:S(2)}) copy-start(u32[32]{0:T(128)} %constant.49) | copy-start | bytes 388
  319.1 7.4 %collective-permute-start.1 = (bf16[6,64]{1,0:T(8,128)(2,1)S(1)}, bf16[6,64]{1,0:T(8,128)(2,1)S(1)}, u32[]{:S(2)}, u32[]{:S(2)}) collective-permute-start(bf16[6,64]{1,0:T(8,128)(2,1)S(1)} %slice.3), channel_id=1, source_target_pairs={{0,4},{4,8},{8,12},{1,5},{5,9},{9,13},{2,6},{6,10},{10,14},{3,7},{... | collective-permute-start | bytes 2312
  323.7 4.7 %collective-permute-start = (f32[6,2048]{1,0:T(8,128)S(1)}, f32[6,2048]{1,0:T(8,128)S(1)}, u32[]{:S(2)}, u32[]{:S(2)}) collective-permute-start(f32[6,2048]{1,0:T(8,128)S(1)} %slice.2), channel_id=1, source_target_pairs={{0,4},{4,8},{8,12},{1,5},{5,9},{9,13},{2,6},{6,10},{10,14},{3,7},{... | collective-permute-start | bytes 147464
Sparse Core Ops, SparseCore 0:
  8.9 22.3 all-gather.5
  184.6 44.3 all-gather.3
where the time goes:
time: 338 us; the launch traced here: 336 us
  other arithmetic  136 us (40%)
  waiting for transfers between devices  71.2 us (21%)
  local copies, waits for them, and re-layouts  63 us (19%)
  blocking collectives  23.4 us (7%)
  matrix products  17.5 us (5%)
  between operations  14.2 us (4%)
  starting transfers between devices  10.5 us (3%)
    unnamed x1, other arithmetic  135 us
    all_to_all x1, waiting for transfers between devices, on_device(): lax.all_to_all(pool_b, 'seq', split_axis=2, concat_axis=0, tiled=True)  68.4 us
    unnamed x24, local copies, waits for them, and re-layouts  53.6 us
    unnamed x1, blocking collectives  23.4 us
    dot_general x1, matrix products, on_device(): jnp.einsum('tf,df->td', masked, w_up, preferred_element_type=jnp.float32)  14.2 us
    all_to_all x1, local copies, waits for them, and re-layouts, on_device(): lax.all_to_all(pool_b, 'seq', split_axis=2, concat_axis=0, tiled=True)  6.82 us
  transfers between devices with their start and end apart: 5, of which 2 were waited for; matrix products, arithmetic and copies ran while one was open for 71% of the time, Pallas kernels for 0%

commit v1 on v0

v1 whole, which is shorter than its diff:
```python
import functools

import jax
import jax.numpy as jnp
from jax import lax
from jax.experimental import pallas as pl
from jax.experimental.pallas import tpu as pltpu
from jax.sharding import PartitionSpec as P

R = 64
TOK_DEV = 30
SEG = 15
PAD = 32
K_CHUNKS = 2
D_TILE = 256
MESH = pl.DeviceIdType.MESH

adapter_scale_factor = 0.5
NT = (((1,), (1,)), ((), ()))


def flip(index, bits):
    result, bit = index, 1
    while bit <= bits:
        if bits & bit:
            result = result + bit - 2 * bit * ((index // bit) % 2)
        bit *= 2
    return result


def kernel(
    ns, nmp, nrep,
    grad_hbm, w_hbm, a_hbm, b_hbm, adapter_ref, slot_ref, len_ref,
    out_ref,
    own_raw, g, w, a, b, acc, low_own, low_in, low_all, low_rows, quant_out, quant_in, scale_out, scale_in,
    own_sem, w_sem, a_sem, b_own_sem,
    gx_send, gx_recv, gs_send, gs_recv, b_send, b_recv,
    l_send, l_recv, m_send, m_recv, q_send, q_recv, c_send, c_recv,
):
    z, x, c = lax.axis_index("seq"), lax.axis_index("mp"), lax.axis_index("rep")
    members = nmp * nrep
    me = x * nrep + c
    blocks = ns
    per_dev = blocks // members
    rank_part = b.shape[1]
    hidden = w.shape[1]
    chunk = hidden // K_CHUNKS
    d_part = w.shape[0]
    tokens = blocks * PAD
    z_order = list(range(ns - 1, 0, -1))
    if ns == 4:
        z_order = [2, 3, 1]

    own_copy = pltpu.make_async_copy(grad_hbm, own_raw, own_sem)
    own_copy.start()

    barrier = pltpu.get_barrier_semaphore()
    for s in z_order:
        pl.semaphore_signal(barrier, inc=1, device_id={"seq": flip(z, s)}, device_id_type=MESH)
    for s in range(1, members):
        peer = flip(me, s)
        pl.semaphore_signal(
            barrier, inc=1, device_id={"mp": peer // nrep, "rep": peer % nrep}, device_id_type=MESH
        )

    def w_copy(t):
        rows = pl.ds(pl.multiple_of(t * D_TILE, D_TILE), D_TILE)
        return pltpu.make_async_copy(w_hbm.at[rows], w.at[rows], w_sem.at[t])

    tiles = d_part // D_TILE
    for t in range(tiles):
        w_copy(t).start()
    a_copy = pltpu.make_async_copy(a_hbm.at[0], a, a_sem)
    a_copy.start()

    own_copy.wait()
    row = lax.broadcasted_iota(jnp.int32, (TOK_DEV, 1), 0)
    second = row >= SEG
    for i in range(per_dev):
        block = me * per_dev + i
        length = jnp.where(second, len_ref[block, 1] + SEG, len_ref[block, 0])
        rows = own_raw[i * TOK_DEV:(i + 1) * TOK_DEV, :]
        rows = jnp.where(row < length, rows.astype(jnp.float32), 0.0).astype(jnp.bfloat16)
        rows = jnp.concatenate([rows, jnp.zeros((PAD - TOK_DEV, hidden), jnp.bfloat16)], axis=0)
        g[me, i] = rows

    pl.semaphore_wait(barrier, ns - 1 + members - 1)

    def b_part(q):
        return b_hbm.at[0, pl.ds(pl.multiple_of(me * rank_part, rank_part), rank_part),
                        pl.ds(pl.multiple_of(q * hidden, hidden), hidden)]

    b_copies = {}
    for s in z_order:
        b_copies[s] = pltpu.make_async_remote_copy(
            src_ref=b_part(flip(z, s)), dst_ref=b.at[s],
            send_sem=b_send.at[s], recv_sem=b_recv.at[s],
            device_id={"seq": flip(z, s)}, device_id_type=MESH)

    def g_part(member, k):
        return g.at[member, :, :, k * chunk:(k + 1) * chunk]

    def g_copy(member, k, send, recv, s, device):
        return pltpu.make_async_remote_copy(
            src_ref=g_part(member, k), dst_ref=g_part(member, k),
            send_sem=send.at[s, k], recv_sem=recv.at[s, k],
            device_id=device, device_id_type=MESH)

    across, beside = {}, {}
    sibling = {"rep": flip(c, 1)}
    for k in range(K_CHUNKS):
        for s in range(1, nmp):
            across[s, k] = g_copy(me, k, gx_send, gx_recv, s, {"mp": flip(x, s)})
            across[s, k].start()
        if k == 0:
            for s in z_order:
                b_copies[s].start()
        beside[0, k] = g_copy(me, k, gs_send, gs_recv, 0, sibling)
        beside[0, k].start()
    b_own = pltpu.make_async_copy(b_part(z), b.at[0], b_own_sem)
    b_own.start()

    for k in range(K_CHUNKS):
        for s in range(1, nmp):
            across[s, k].wait_recv()
            beside[s, k] = g_copy(flip(x, s) * nrep + c, k, gs_send, gs_recv, s, sibling)
            beside[s, k].start()
        for s in range(nmp):
            beside[s, k].wait_recv()

        def tile_step(t, carry, k=k):
            rows = pl.ds(pl.multiple_of(t * D_TILE, D_TILE), D_TILE)
            if k == 0:
                w_copy(t).wait()
            part = lax.dot_general(
                g[:, :, :, k * chunk:(k + 1) * chunk].reshape(tokens, chunk),
                w[rows, k * chunk:(k + 1) * chunk], NT,
                preferred_element_type=jnp.float32)
            if k == 0:
                acc[:, rows] = part
            else:
                acc[:, rows] += part
            return carry

        lax.fori_loop(0, tiles, tile_step, 0)

    lane = lax.broadcasted_iota(jnp.int32, (1, tokens), 1)
    slots = jnp.zeros((1, tokens), jnp.int32)
    for block in range(blocks):
        for j in range(2):
            slot = slot_ref[adapter_ref[block, j]]
            slots = jnp.where(lane >= block * PAD + j * SEG, slot, slots)

    masked = g[...].reshape(tokens, hidden)
    picked = jnp.zeros((rank_part, tokens), jnp.float32)
    for s in [0] + z_order[::-1]:
        if s == 0:
            b_own.wait()
        else:
            b_copies[s].wait_recv()
        every = lax.dot_general(b[s], masked, NT, preferred_element_type=jnp.float32)
        picked = jnp.where(slots == flip(z, s), every, picked)
    low_own[...] = picked

    low_copies = []
    for s in z_order:
        low_copies.append(pltpu.make_async_remote_copy(
            src_ref=low_own, dst_ref=low_in.at[s], send_sem=l_send.at[s], recv_sem=l_recv.at[s],
            device_id={"seq": flip(z, s)}, device_id_type=MESH))
        low_copies[-1].start()
    total = picked
    for s, copy in zip(z_order, low_copies):
        copy.wait_recv()
        total = total + low_in[s]
    low_all[me] = (adapter_scale_factor * total).astype(jnp.bfloat16)

    member_copies = []
    for s in range(members - 1, 0, -1):
        peer = flip(me, s)
        member_copies.append(pltpu.make_async_remote_copy(
            src_ref=low_all.at[me], dst_ref=low_all.at[me], send_sem=m_send.at[s], recv_sem=m_recv.at[s],
            device_id={"mp": peer // nrep, "rep": peer % nrep}, device_id_type=MESH))
        member_copies[-1].start()
    for copy in member_copies:
        copy.wait_recv()
    a_copy.wait()

    low_t = low_all[...].astype(jnp.float32).reshape(members * rank_part, tokens)
    low_t = jnp.where(slots == z, low_t, 0.0)
    low_rows[...] = low_t.T.astype(jnp.bfloat16)

    def block_sum(block):
        rows = pl.ds(pl.multiple_of(block * PAD, PAD), PAD)
        low_term = lax.dot_general(low_rows[rows, :], a[...], NT, preferred_element_type=jnp.float32)
        return acc[rows, :] + low_term

    groups = d_part // 128
    out_copies = []
    for s in z_order:
        dest = flip(z, s)
        value = block_sum(dest)
        largest = jnp.abs(value[:, :128])
        for i in range(1, groups):
            largest = jnp.maximum(largest, jnp.abs(value[:, i * 128:(i + 1) * 128]))
        largest = jnp.max(largest.reshape(PAD // 8, 8, 128), axis=0)
        largest = jnp.maximum(largest, 1e-33)
        scale_out[s] = largest * (1.0 / 32767.0)
        inverse = jnp.tile(32767.0 / largest, (PAD // 8, 1))
        for i in range(groups):
            q = jnp.round(value[:, i * 128:(i + 1) * 128] * inverse)
            quant_out[s, :, i * 128:(i + 1) * 128] = q.astype(jnp.int32).astype(jnp.int16)
        for src, dst, send, recv in ((quant_out, quant_in, q_send, q_recv), (scale_out, scale_in, c_send, c_recv)):
            copy = pltpu.make_async_remote_copy(
                src_ref=src.at[s], dst_ref=dst.at[s], send_sem=send.at[s], recv_sem=recv.at[s],
                device_id={"seq": dest}, device_id_type=MESH)
            copy.start()
            out_copies.append(copy)

    rows = pl.ds(pl.multiple_of(z * PAD, PAD), PAD)
    acc[rows, :] = block_sum(z)
    for copy in out_copies:
        copy.wait_recv()
    scales = {s: jnp.tile(scale_in[s], (PAD // 8, 1)) for s in z_order}
    for i in range(groups):
        columns = slice(i * 128, (i + 1) * 128)
        result = acc[rows, columns]
        for s in z_order:
            result = result + quant_in[s, :, columns].astype(jnp.int32).astype(jnp.float32) * scales[s]
        out_ref[:, columns] = result[:TOK_DEV].astype(jnp.bfloat16)

    for copy in [*b_copies.values(), *across.values(), *beside.values(), *low_copies, *member_copies, *out_copies]:
        copy.wait_send()


def on_device(ns, nmp, nrep, grad_hidden, w_up, pool_a, pool_b, seg_adapter, adapter_slot, seg_len):
    members = nmp * nrep
    d_part, hidden = w_up.shape
    rank_part = R // members
    tokens = ns * PAD
    hbm = pl.BlockSpec(memory_space=pl.ANY)
    smem = pl.BlockSpec(memory_space=pltpu.SMEM)
    dma = pltpu.SemaphoreType.DMA
    bf16, f32 = jnp.bfloat16, jnp.float32
    scratch = [
        pltpu.VMEM(grad_hidden.shape, bf16),
        pltpu.VMEM((members, ns // members, PAD, hidden), bf16),
        pltpu.VMEM(w_up.shape, bf16),
        pltpu.VMEM((d_part, R), bf16),
        pltpu.VMEM((ns, rank_part, hidden), bf16),
        pltpu.VMEM((tokens, d_part), f32),
        pltpu.VMEM((rank_part, tokens), f32),
        pltpu.VMEM((ns, rank_part, tokens), f32),
        pltpu.VMEM((members, rank_part, tokens), bf16),
        pltpu.VMEM((tokens, R), bf16),
        pltpu.VMEM((ns, PAD, d_part), jnp.int16),
        pltpu.VMEM((ns, PAD, d_part), jnp.int16),
        pltpu.VMEM((ns, 8, 128), f32),
        pltpu.VMEM((ns, 8, 128), f32),
        dma, dma((d_part // D_TILE,)), dma, dma,
        dma((nmp, K_CHUNKS)), dma((nmp, K_CHUNKS)), dma((nmp, K_CHUNKS)), dma((nmp, K_CHUNKS)),
        dma((ns,)), dma((ns,)),
        dma((ns,)), dma((ns,)), dma((members,)), dma((members,)),
        dma((ns,)), dma((ns,)), dma((ns,)), dma((ns,)),
    ]
    return pl.pallas_call(
        functools.partial(kernel, ns, nmp, nrep),
        out_shape=jax.ShapeDtypeStruct((TOK_DEV, d_part), bf16),
        in_specs=[hbm] * 4 + [smem] * 3,
        out_specs=pl.BlockSpec(memory_space=pltpu.VMEM),
        scratch_shapes=scratch,
        compiler_params=pltpu.CompilerParams(
            collective_id=0, has_side_effects=True, vmem_limit_bytes=56 * 1024 * 1024
        ),
        cost_estimate=pl.CostEstimate(
            flops=2 * tokens * d_part * hidden, bytes_accessed=2 * d_part * hidden, transcendentals=0
        ),
    )(grad_hidden, w_up, pool_a, pool_b, seg_adapter, adapter_slot, seg_len)


def solution(mesh):
    ns, nmp, nrep = mesh.shape["seq"], mesh.shape["mp"], mesh.shape["rep"]
    in_specs = (
        P(("groups", "mp", "rep"), "seq"),
        P(("mp", "rep"), "seq"),
        P(("groups", "seq"), ("mp", "rep"), None),
        P(("groups", "seq"), None, None),
        P("groups", None),
        P("groups"),
        P("groups", None),
    )
    out_specs = P(("groups", "seq"), ("mp", "rep"))
    return jax.shard_map(
        functools.partial(on_device, ns, nmp, nrep),
        mesh=mesh, in_specs=in_specs, out_specs=out_specs, check_vma=False,
    )
```

time: 338 us -> 54.7 us (0.16)
  other arithmetic: 136 us -> 0 us
  waiting for transfers between devices: 71.2 us -> 0 us
  local copies, waits for them, and re-layouts: 63 us -> 6.15 us
  Pallas kernels: 0 us -> 48.4 us
  blocking collectives: 23.4 us -> 0 us
  matrix products: 17.5 us -> 0 us
  between operations: 14.2 us -> 0.01 us
  starting transfers between devices: 10.5 us -> 0 us
    unnamed x1 -> x0, other arithmetic: 135 us -> none
    all_to_all x1 -> x0, waiting for transfers between devices: 68.4 us -> none  [on_device(): lax.all_to_all(pool_b, 'seq', split_axis=2, concat_axis=0, tiled=True)]
    pallas_call x0 -> x1, Pallas kernels: none -> 48.4 us  [on_device(): pl.pallas_call(functools.partial(kernel, ns, nmp, nrep), out_shape=jax.Sh...]
    unnamed x24 -> x4, local copies, waits for them, and re-layouts: 53.6 us -> 6.15 us
    unnamed x1 -> x0, blocking collectives: 23.4 us -> none
    dot_general x3 -> x0, matrix products: 17.5 us -> none  [the longest x1 14.2 us: on_device(): jnp.einsum('tf,df->td', masked, w_up, preferred_element_type=jnp.float32)]
    all_to_all x1 -> x0, local copies, waits for them, and re-layouts: 6.82 us -> none  [on_device(): lax.all_to_all(pool_b, 'seq', split_axis=2, concat_axis=0, tiled=True)]
    all_to_all x1 -> x0, starting transfers between devices: 6.45 us -> none  [on_device(): lax.all_to_all(pool_b, 'seq', split_axis=2, concat_axis=0, tiled=True)]
  transfers between devices with their start and end apart: 5 -> 0, of which waited for: 2 -> 0; matrix products, arithmetic and copies ran while one was open for 71% -> 0% of each run, Pallas kernels for 0% -> 0%
where the time goes in v1:
time: 54.7 us; the launch traced here: 54.5 us
  Pallas kernels  48.4 us (88%)
  local copies, waits for them, and re-layouts  6.15 us (11%)
    pallas_call x1, Pallas kernels, on_device(): pl.pallas_call(functools.partial(kernel, ns, nmp, nrep), out_shape=jax.Sh...  48.4 us
    unnamed x4, local copies, waits for them, and re-layouts  6.15 us

profile of v1, /device:TPU:0, one launch (start us, length us, event | category | flops | bytes accessed | tf_op | source)
XLA Modules:
  0.0 54.5 jit_solution(7886194007613363706)
XLA Ops:
  0.0 1.3 %copy.9.adapter_ref = s32[4,2]{1,0:T(4,128)} copy(s32[4,2]{0,1:T(2,128)} %param.11) | data formatting | bytes 64 | tf_op args[4]
  1.3 1.3 %copy.10.len_ref = s32[4,2]{1,0:T(4,128)} copy(s32[4,2]{0,1:T(2,128)} %param.13) | data formatting | bytes 64 | tf_op args[6]
  2.6 1.9 %copy.8.a_hbm = bf16[1,2048,64]{2,1,0:T(8,128)(2,1)} copy(bf16[1,2048,64]{1,2,0:T(8,128)(2,1)} %param.9) | data formatting | bytes 524288 | tf_op args[2]
  4.6 48.4 %shard_map.73 = bf16[30,2048]{1,0:T(8,128)(2,1)} custom-call(bf16[30,6144]{1,0:T(8,128)(2,1)} %grad_hbm.1, bf16[2048,6144]{1,0:T(8,128)(2,1)} %w_hbm.1, bf16[1,2048,64]{2,1,0:T(8,128)(2,1)} %copy.8.a_hbm, bf16[1,64,24576]{2,1,0:T(8,128)(2,1)} %b_hbm.1, s32[4,2]{1,0:T(4,128)} %copy.9.adapter_ref, s32[4]{0:T(128)} %slot_ref.1, s32[4,2]{1,0:T(4,128)} %copy.10.len_ref), custom_call_target="tpu_custom_call" | custom-call | flops 3221225472 | bytes 25165824 | tf_op jit(solution)/shard_map/pallas_call | solution.py:265
  52.9 1.6 %copy.12 = bf16[30,2048]{1,0:T(8,128)(2,1)} copy(bf16[30,2048]{1,0:T(8,128)(2,1)} %shard_map.73) | data formatting | bytes 245760

commit v2 on v1

--- a/solution.py
+++ b/solution.py
@@ -32,7 +32,7 @@
     ns, nmp, nrep,
     grad_hbm, w_hbm, a_hbm, b_hbm, adapter_ref, slot_ref, len_ref,
     out_ref,
-    own_raw, g, w, a, b, acc, low_own, low_in, low_all, low_rows, quant_out, quant_in, scale_out, scale_in,
+    own_raw, g, w, a, b, acc, low_out, low_in, low_all, low_rows, quant_out, quant_in, scale_out, scale_in,
     own_sem, w_sem, a_sem, b_own_sem,
     gx_send, gx_recv, gs_send, gs_recv, b_send, b_recv,
     l_send, l_recv, m_send, m_recv, q_send, q_recv, c_send, c_recv,
@@ -68,21 +68,7 @@
         return pltpu.make_async_copy(w_hbm.at[rows], w.at[rows], w_sem.at[t])
 
     tiles = d_part // D_TILE
-    for t in range(tiles):
-        w_copy(t).start()
     a_copy = pltpu.make_async_copy(a_hbm.at[0], a, a_sem)
-    a_copy.start()
-
-    own_copy.wait()
-    row = lax.broadcasted_iota(jnp.int32, (TOK_DEV, 1), 0)
-    second = row >= SEG
-    for i in range(per_dev):
-        block = me * per_dev + i
-        length = jnp.where(second, len_ref[block, 1] + SEG, len_ref[block, 0])
-        rows = own_raw[i * TOK_DEV:(i + 1) * TOK_DEV, :]
-        rows = jnp.where(row < length, rows.astype(jnp.float32), 0.0).astype(jnp.bfloat16)
-        rows = jnp.concatenate([rows, jnp.zeros((PAD - TOK_DEV, hidden), jnp.bfloat16)], axis=0)
-        g[me, i] = rows
 
     pl.semaphore_wait(barrier, ns - 1 + members - 1)
 
@@ -96,6 +82,18 @@
             src_ref=b_part(flip(z, s)), dst_ref=b.at[s],
             send_sem=b_send.at[s], recv_sem=b_recv.at[s],
             device_id={"seq": flip(z, s)}, device_id_type=MESH)
+        b_copies[s].start()
+
+    own_copy.wait()
+    row = lax.broadcasted_iota(jnp.int32, (TOK_DEV, 1), 0)
+    second = row >= SEG
+    for i in range(per_dev):
+        block = me * per_dev + i
+        length = jnp.where(second, len_ref[1, block] + SEG, len_ref[0, block])
+        rows = own_raw[i * TOK_DEV:(i + 1) * TOK_DEV, :]
+        rows = jnp.where(row < length, rows.astype(jnp.float32), 0.0).astype(jnp.bfloat16)
+        rows = jnp.concatenate([rows, jnp.zeros((PAD - TOK_DEV, hidden), jnp.bfloat16)], axis=0)
+        g[me, i] = rows
 
     def g_part(member, k):
         return g.at[member, :, :, k * chunk:(k + 1) * chunk]
@@ -112,23 +110,16 @@
         for s in range(1, nmp):
             across[s, k] = g_copy(me, k, gx_send, gx_recv, s, {"mp": flip(x, s)})
             across[s, k].start()
-        if k == 0:
-            for s in z_order:
-                b_copies[s].start()
         beside[0, k] = g_copy(me, k, gs_send, gs_recv, 0, sibling)
         beside[0, k].start()
     b_own = pltpu.make_async_copy(b_part(z), b.at[0], b_own_sem)
     b_own.start()
-
-    for k in range(K_CHUNKS):
-        for s in range(1, nmp):
-            across[s, k].wait_recv()
-            beside[s, k] = g_copy(flip(x, s) * nrep + c, k, gs_send, gs_recv, s, sibling)
-            beside[s, k].start()
-        for s in range(nmp):
-            beside[s, k].wait_recv()
-
-        def tile_step(t, carry, k=k):
+    for t in range(tiles):
+        w_copy(t).start()
+    a_copy.start()
+
+    def frozen(k, first, last):
+        def tile_step(t, carry):
             rows = pl.ds(pl.multiple_of(t * D_TILE, D_TILE), D_TILE)
             if k == 0:
                 w_copy(t).wait()
@@ -142,34 +133,45 @@
                 acc[:, rows] += part
             return carry
 
-        lax.fori_loop(0, tiles, tile_step, 0)
+        lax.fori_loop(first, last, tile_step, 0)
+
+    for k in range(K_CHUNKS):
+        for s in range(1, nmp):
+            across[s, k].wait_recv()
+            beside[s, k] = g_copy(flip(x, s) * nrep + c, k, gs_send, gs_recv, s, sibling)
+            beside[s, k].start()
+        for s in range(nmp):
+            beside[s, k].wait_recv()
+        if k < K_CHUNKS - 1:
+            frozen(k, 0, tiles)
 
     lane = lax.broadcasted_iota(jnp.int32, (1, tokens), 1)
     slots = jnp.zeros((1, tokens), jnp.int32)
     for block in range(blocks):
         for j in range(2):
-            slot = slot_ref[adapter_ref[block, j]]
+            slot = slot_ref[adapter_ref[j, block]]
             slots = jnp.where(lane >= block * PAD + j * SEG, slot, slots)
 
-    masked = g[...].reshape(tokens, hidden)
-    picked = jnp.zeros((rank_part, tokens), jnp.float32)
-    for s in [0] + z_order[::-1]:
-        if s == 0:
-            b_own.wait()
-        else:
-            b_copies[s].wait_recv()
-        every = lax.dot_general(b[s], masked, NT, preferred_element_type=jnp.float32)
-        picked = jnp.where(slots == flip(z, s), every, picked)
-    low_own[...] = picked
-
+    def low_part(s):
+        every = lax.dot_general(
+            b[s], g[...].reshape(tokens, hidden), NT, preferred_element_type=jnp.float32)
+        return jnp.where(slots == flip(z, s), every, 0.0)
+
+    b_own.wait()
+    total = low_part(0)
+    last = K_CHUNKS - 1
     low_copies = []
-    for s in z_order:
+    for s in range(1, ns):
+        if s == min(2, ns - 1):
+            frozen(last, 0, tiles // 2)
+        b_copies[s].wait_recv()
+        low_out[s] = low_part(s)
         low_copies.append(pltpu.make_async_remote_copy(
-            src_ref=low_own, dst_ref=low_in.at[s], send_sem=l_send.at[s], recv_sem=l_recv.at[s],
+            src_ref=low_out.at[s], dst_ref=low_in.at[s], send_sem=l_send.at[s], recv_sem=l_recv.at[s],
             device_id={"seq": flip(z, s)}, device_id_type=MESH))
         low_copies[-1].start()
-    total = picked
-    for s, copy in zip(z_order, low_copies):
+    frozen(last, tiles // 2, tiles * 3 // 4)
+    for s, copy in enumerate(low_copies, 1):
         copy.wait_recv()
         total = total + low_in[s]
     low_all[me] = (adapter_scale_factor * total).astype(jnp.bfloat16)
@@ -181,17 +183,17 @@
             src_ref=low_all.at[me], dst_ref=low_all.at[me], send_sem=m_send.at[s], recv_sem=m_recv.at[s],
             device_id={"mp": peer // nrep, "rep": peer % nrep}, device_id_type=MESH))
         member_copies[-1].start()
+    frozen(last, tiles * 3 // 4, tiles)
     for copy in member_copies:
         copy.wait_recv()
     a_copy.wait()
 
     low_t = low_all[...].astype(jnp.float32).reshape(members * rank_part, tokens)
-    low_t = jnp.where(slots == z, low_t, 0.0)
     low_rows[...] = low_t.T.astype(jnp.bfloat16)
 
     def block_sum(block):
         rows = pl.ds(pl.multiple_of(block * PAD, PAD), PAD)
-        low_term = lax.dot_general(low_rows[rows, :], a[...], NT, preferred_element_type=jnp.float32)
+        low_term = jnp.dot(low_rows[rows, :], a[...], preferred_element_type=jnp.float32)
         return acc[rows, :] + low_term
 
     groups = d_part // 128
@@ -245,10 +247,10 @@
         pltpu.VMEM(grad_hidden.shape, bf16),
         pltpu.VMEM((members, ns // members, PAD, hidden), bf16),
         pltpu.VMEM(w_up.shape, bf16),
-        pltpu.VMEM((d_part, R), bf16),
+        pltpu.VMEM((R, d_part), bf16),
         pltpu.VMEM((ns, rank_part, hidden), bf16),
         pltpu.VMEM((tokens, d_part), f32),
-        pltpu.VMEM((rank_part, tokens), f32),
+        pltpu.VMEM((ns, rank_part, tokens), f32),
         pltpu.VMEM((ns, rank_part, tokens), f32),
         pltpu.VMEM((members, rank_part, tokens), bf16),
         pltpu.VMEM((tokens, R), bf16),
@@ -274,7 +276,7 @@
         cost_estimate=pl.CostEstimate(
             flops=2 * tokens * d_part * hidden, bytes_accessed=2 * d_part * hidden, transcendentals=0
         ),
-    )(grad_hidden, w_up, pool_a, pool_b, seg_adapter, adapter_slot, seg_len)
+    )(grad_hidden, w_up, jnp.swapaxes(pool_a, 1, 2), pool_b, seg_adapter.T, adapter_slot, seg_len.T)
 
 
 def solution(mesh):

time: 54.7 us -> 46.6 us (0.85)
  local copies, waits for them, and re-layouts: 6.15 us -> 1.57 us
  Pallas kernels: 48.4 us -> 44.8 us
    unnamed x4 -> x1, local copies, waits for them, and re-layouts: 6.15 us -> 1.57 us
    pallas_call x1, Pallas kernels: 48.4 us -> 44.8 us  [on_device(): pl.pallas_call(functools.partial(kernel, ns, nmp, nrep), out_shape=jax.Sh...]
where the time goes in v2:
time: 46.6 us; the launch traced here: 46.4 us
  Pallas kernels  44.8 us (96%)
  local copies, waits for them, and re-layouts  1.57 us (3%)
    pallas_call x1, Pallas kernels, on_device(): pl.pallas_call(functools.partial(kernel, ns, nmp, nrep), out_shape=jax.Sh...  44.8 us
    unnamed x1, local copies, waits for them, and re-layouts  1.57 us

profile of v2, /device:TPU:0, one launch (start us, length us, event | category | flops | bytes accessed | tf_op | source)
XLA Modules:
  0.0 46.4 jit_solution(13622059715409457442)
XLA Ops:
  0.0 44.8 %shard_map.73 = bf16[30,2048]{1,0:T(8,128)(2,1)} custom-call(bf16[30,6144]{1,0:T(8,128)(2,1)} %grad_hbm.1, bf16[2048,6144]{1,0:T(8,128)(2,1)} %w_hbm.1, bf16[1,64,2048]{2,1,0:T(8,128)(2,1)} %bitcast.3, bf16[1,64,24576]{2,1,0:T(8,128)(2,1)} %b_hbm.1, s32[2,4]{1,0:T(2,128)} %bitcast.4, s32[4]{0:T(128)} %slot_ref.1, s32[2,4]{1,0:T(2,128)} %bitcast.5), custom_call_target="tpu_custom_call" | custom-call | flops 3221225472 | bytes 25165824 | tf_op jit(solution)/shard_map/pallas_call | solution.py:267
  44.8 1.6 %copy.9 = bf16[30,2048]{1,0:T(8,128)(2,1)} copy(bf16[30,2048]{1,0:T(8,128)(2,1)} %shard_map.73) | data formatting | bytes 245760

commit v3 on v2

--- a/solution.py
+++ b/solution.py
@@ -163,14 +163,14 @@
     low_copies = []
     for s in range(1, ns):
         if s == min(2, ns - 1):
-            frozen(last, 0, tiles // 2)
+            frozen(last, 0, tiles // 4)
         b_copies[s].wait_recv()
         low_out[s] = low_part(s)
         low_copies.append(pltpu.make_async_remote_copy(
             src_ref=low_out.at[s], dst_ref=low_in.at[s], send_sem=l_send.at[s], recv_sem=l_recv.at[s],
             device_id={"seq": flip(z, s)}, device_id_type=MESH))
         low_copies[-1].start()
-    frozen(last, tiles // 2, tiles * 3 // 4)
+    frozen(last, tiles // 4, tiles * 5 // 8)
     for s, copy in enumerate(low_copies, 1):
         copy.wait_recv()
         total = total + low_in[s]
@@ -183,7 +183,7 @@
             src_ref=low_all.at[me], dst_ref=low_all.at[me], send_sem=m_send.at[s], recv_sem=m_recv.at[s],
             device_id={"mp": peer // nrep, "rep": peer % nrep}, device_id_type=MESH))
         member_copies[-1].start()
-    frozen(last, tiles * 3 // 4, tiles)
+    frozen(last, tiles * 5 // 8, tiles)
     for copy in member_copies:
         copy.wait_recv()
     a_copy.wait()

time: 46.6 us -> 45.2 us (0.970)
  Pallas kernels: 44.8 us -> 43.5 us
    pallas_call x1, Pallas kernels: 44.8 us -> 43.5 us  [on_device(): pl.pallas_call(functools.partial(kernel, ns, nmp, nrep), out_shape=jax.Sh...]
where the time goes in v3:
time: 45.2 us; the launch traced here: 45.1 us
  Pallas kernels  43.5 us (96%)
  local copies, waits for them, and re-layouts  1.57 us (3%)
    pallas_call x1, Pallas kernels, on_device(): pl.pallas_call(functools.partial(kernel, ns, nmp, nrep), out_shape=jax.Sh...  43.5 us
    unnamed x1, local copies, waits for them, and re-layouts  1.57 us

profile of v3, /device:TPU:0, one launch (start us, length us, event | category | flops | bytes accessed | tf_op | source)
XLA Modules:
  0.0 45.1 jit_solution(15818206095981927733)
XLA Ops:
  0.0 43.5 %shard_map.73 = bf16[30,2048]{1,0:T(8,128)(2,1)} custom-call(bf16[30,6144]{1,0:T(8,128)(2,1)} %grad_hbm.1, bf16[2048,6144]{1,0:T(8,128)(2,1)} %w_hbm.1, bf16[1,64,2048]{2,1,0:T(8,128)(2,1)} %bitcast.3, bf16[1,64,24576]{2,1,0:T(8,128)(2,1)} %b_hbm.1, s32[2,4]{1,0:T(2,128)} %bitcast.4, s32[4]{0:T(128)} %slot_ref.1, s32[2,4]{1,0:T(2,128)} %bitcast.5), custom_call_target="tpu_custom_call" | custom-call | flops 3221225472 | bytes 25165824 | tf_op jit(solution)/shard_map/pallas_call | solution.py:267
  43.5 1.6 %copy.9 = bf16[30,2048]{1,0:T(8,128)(2,1)} copy(bf16[30,2048]{1,0:T(8,128)(2,1)} %shard_map.73) | data formatting | bytes 245760
